TPU v7x, 256 devices: a whole 4x4x8 slice. The times are simulated.
256 devices in a mesh: seq: 64 (over z, x, core), tp: 4 (over y).
Axes of the slice: x: 4, y: 4, z: 8, core: 2. Of those that a mesh axis runs over, the one named last changes fastest.
Arguments:
- tokens: bfloat16 [32768, 4096], P('seq', 'tp'), may hold values from -6 to 6
- log_decay: float32 [32768, 16], P('seq', 'tp'), may hold values from -2 to 0
- w_query: bfloat16 [4096, 2048], P(None, 'tp'), may hold values from -0.09375 to 0.09375
- w_key: bfloat16 [4096, 512], P(None, 'tp'), may hold values from -0.09375 to 0.09375
- w_value: bfloat16 [4096, 512], P(None, 'tp'), may hold values from -0.09375 to 0.09375
- w_level: bfloat16 [4096, 144], P(None, 'tp'), may hold values from -0.09375 to 0.09375
- w_out: bfloat16 [2048, 4096], P('tp'), may hold values from -0.125 to 0.125
Outputs:
- mixed: bfloat16 [32768, 4096], P('seq', 'tp')
All inputs are finite; a program needn't handle non-finite values.
Results may differ from a plain program's by a relative error of at most 0.02.
Values may be sent and summed in bfloat16 or wider, within the bound.
A program may use at most 128 MiB of HBM per device.

v0:
```python
import jax
import jax.numpy as jnp
from jax import lax
from jax.sharding import PartitionSpec as P

BLOCK = 128
HIGHEST = lax.Precision.HIGHEST


def prefix(part, axis, combine, identity):
    place = lax.axis_index(axis)
    gathered = lax.all_gather(part, axis)
    state = jnp.zeros_like(part) + jnp.asarray(identity, part.dtype)

    def one(step, state):
        return combine(state, lax.dynamic_index_in_dim(gathered, step, 0, False))

    return lax.fori_loop(0, place, one, state)


def top_bit(differ, bit_count):
    result = jnp.zeros_like(differ)
    for shift in range(1, bit_count):
        result = result + (jnp.right_shift(differ, shift) > 0).astype(jnp.int32)
    return result


def split_pair(wide):
    upper_part = wide.astype(jnp.bfloat16)
    lower_part = (wide - upper_part.astype(jnp.float32)).astype(jnp.bfloat16)
    return (upper_part, lower_part)


def body(tokens, log_decay, w_query, w_key, w_value, w_level, w_out):
    rows = tokens.shape[0]
    heads_local = log_decay.shape[1]
    head_size = w_out.shape[0] // heads_local
    level_count = w_level.shape[1] // heads_local
    kv_local = w_key.shape[1] // head_size
    group_size = heads_local // kv_local
    matrices = (w_query, w_key, w_value, w_level)
    piece = lax.all_gather(tokens, "tp", axis=1, tiled=True)
    sums = tuple(
        (jnp.dot(piece, matrix, preferred_element_type=jnp.float32) for matrix in matrices)
    )
    query = sums[0].astype(jnp.bfloat16).reshape(rows, kv_local, group_size, head_size)
    keys_here = sums[1].astype(jnp.bfloat16).reshape(rows, kv_local, head_size)
    values_here = sums[2].astype(jnp.bfloat16).reshape(rows, kv_local, head_size)
    level_weight = jax.nn.softplus(sums[3]).reshape(rows, heads_local, level_count)
    decay_sum = jnp.cumsum(log_decay, axis=0)
    slab_total = decay_sum[rows - 1]
    before = prefix(slab_total, "seq", jnp.add, jnp.zeros_like(slab_total))
    ends_here = before + slab_total
    positions = jnp.arange(rows, dtype=jnp.int32)
    block_of = positions // BLOCK
    local_bits = (rows // BLOCK).bit_length() - 1
    block_differ = jnp.bitwise_xor(block_of[:, None], block_of[None, :])
    level_table = jnp.where(block_differ == 0, 0, 1 + top_bit(block_differ, local_bits))
    causal = positions[:, None] >= positions[None, :]
    decay_heads = decay_sum.T
    gaps = jnp.where(causal[None], decay_heads[:, :, None] - decay_heads[:, None, :], -jnp.inf)
    picked = jnp.zeros((heads_local, rows, rows), jnp.float32)
    for level in range(local_bits + 1):
        picked = picked + jnp.where(
            level_table[None] == level, level_weight[:, :, level].T[:, :, None], 0.0
        )
    scores = jnp.einsum(
        "tgqd,sgd->gqts", query, keys_here, preferred_element_type=jnp.float32
    ).reshape(heads_local, rows, rows)
    mixing = (picked * jnp.exp(gaps) * scores).reshape(kv_local, group_size, rows, rows)
    mixing_upper, mixing_lower = split_pair(mixing)
    local_part = jnp.einsum(
        "gqts,sgd->gqtd", mixing_upper, values_here, preferred_element_type=jnp.float32
    )
    local_part = local_part + jnp.einsum(
        "gqts,sgd->gqtd", mixing_lower, values_here, preferred_element_type=jnp.float32
    )
    local_part = local_part.reshape(heads_local, rows, head_size)
    keep_factor = jnp.exp(slab_total[None, :] - decay_sum).reshape(rows, kv_local, group_size)
    weighted_keys = keep_factor[:, :, :, None] * keys_here.astype(jnp.float32)[:, :, None, :]
    keys_upper, keys_lower = split_pair(weighted_keys)
    own_state = jnp.einsum(
        "tgqd,tge->gqde", keys_upper, values_here, preferred_element_type=jnp.float32
    )
    own_state = own_state + jnp.einsum(
        "tgqd,tge->gqde", keys_lower, values_here, preferred_element_type=jnp.float32
    )
    own_state = own_state.reshape(heads_local, head_size, head_size)
    seq_bits = lax.axis_size("seq").bit_length() - 1
    device = lax.axis_index("seq")
    empty = jnp.zeros((seq_bits, heads_local, head_size, head_size), jnp.float32)
    states = lax.all_gather(own_state[None], "seq", axis=0, tiled=True)
    slab_ends = lax.all_gather(ends_here[None], "seq", axis=0, tiled=True)
    sources = jnp.arange(states.shape[0], dtype=jnp.int32)
    earlier = sources < device
    highest_bit = top_bit(jnp.bitwise_xor(sources, device), seq_bits)
    onehot = jnp.logical_and(
        highest_bit[:, None] == jnp.arange(seq_bits, dtype=jnp.int32)[None, :], earlier[:, None]
    ).astype(jnp.float32)
    fading = jnp.exp(jnp.where(earlier[:, None], before[None, :] - slab_ends, -jnp.inf))
    buckets = empty + jnp.einsum("nb,nh,nhde->bhde", onehot, fading, states, precision=HIGHEST)
    query_heads = query.reshape(rows, heads_local, head_size)
    buckets_upper, buckets_lower = split_pair(buckets)
    per_level = jnp.einsum(
        "thd,bhde->bthe", query_heads, buckets_upper, preferred_element_type=jnp.float32
    )
    per_level = per_level + jnp.einsum(
        "thd,bhde->bthe", query_heads, buckets_lower, preferred_element_type=jnp.float32
    )
    span_weight = (
        level_weight[:, :, local_bits + 1 : local_bits + 1 + seq_bits]
        * jnp.exp(decay_sum)[:, :, None]
    )
    remote_part = jnp.einsum("bthe,thb->hte", per_level, span_weight, precision=HIGHEST)
    combined = local_part + remote_part
    normed = (
        combined * lax.rsqrt(jnp.mean(combined * combined, axis=-1, keepdims=True) + 1e-05)
    ).astype(jnp.bfloat16)
    partial_out = jnp.einsum(
        "htd,hde->te",
        normed,
        w_out.reshape(heads_local, head_size, w_out.shape[1]),
        preferred_element_type=jnp.float32,
    )
    return lax.psum_scatter(partial_out.astype(jnp.bfloat16), "tp", scatter_dimension=1, tiled=True)


def solution(mesh):
    in_specs = (
        P("seq", "tp"),
        P("seq", "tp"),
        P(None, "tp"),
        P(None, "tp"),
        P(None, "tp"),
        P(None, "tp"),
        P("tp", None),
    )
    out_specs = P("seq", "tp")
    return jax.shard_map(body, mesh=mesh, in_specs=in_specs, out_specs=out_specs, check_vma=False)
```

profile of v0, /device:TPU:1, one launch (start us, length us, event | category | flops | bytes accessed | tf_op | source)
XLA Modules:
  0.0 341.4 jit_solution(4485512293242226166)
XLA Ops:
  6.5 0.7 all-gather.6.cloned.1.call-update
  7.3 0.7 reshape.296
  8.0 1.2 reduce-window.6
  9.9 53.9 %all-gather.6.cloned.1.call-done = bf16[512,4096]{1,0:T(8,128)(2,1)} async-done(((bf16[512,1024]{1,0:T(8,128)(2,1)}), bf16[512,4096]{1,0:T(8,128)(2,1)}) %all-gather.6.cloned.1.call-update) | async-done | bytes 4194320 | tf_op jit(solution)/shard_map/all_gather | solution.py:42
  63.8 3.4 %convolution_convert_fusion.2 = bf16[512,128]{1,0:T(8,128)(2,1)S(1)} fusion(bf16[512,4096]{1,0:T(8,128)(2,1)} %all-gather.6.cloned.1.call-done, bf16[4096,128]{1,0:T(8,128)(2,1)S(1)} %copy-done), kind=kOutput, calls=%fused_computation.24 | convolution fusion | flops 536936448 | bytes 5373952 | tf_op jit(solution)/shard_map/dot_general | solution.py:44
  67.4 3.8 %fusion.14 = bf16[512,128,1]{1,0,2:T(8,128)(2,1)S(1)} fusion(bf16[512,4096]{1,0:T(8,128)(2,1)} %all-gather.6.cloned.1.call-done, bf16[4096,128]{1,0:T(8,128)(2,1)} %param.13), kind=kOutput, calls=%fused_computation.25 | convolution fusion | flops 536936448 | bytes 5373952 | tf_op jit(solution)/shard_map/dot_general | solution.py:44
  71.5 1.0 convolution_add_fusion
  73.9 41.7 %all-gather.2 = f32[64,1,4]{2,1,0:T(1,128)S(1)} all-gather(f32[1,1,4]{2,1,0:T(1,128)S(1)} %bitcast.109), channel_id=1, replica_groups=mesh['seq'=64,'tp'=4] {'seq'}, dimensions={0}, use_global_device_ids=true | all-gather | bytes 1040 | tf_op jit(solution)/shard_map/all_gather | solution.py:12
  115.8 124.5 %all-reduce = f32[256]{0:T(256)S(1)} all-reduce(f32[256]{0:T(256)S(1)} %add_dynamic-update-slice_fusion), channel_id=2, replica_groups=mesh['seq'=64,'tp'=4] {'seq'}, use_global_device_ids=true, to_apply=%add | all-reduce | flops 256 | bytes 2048
  240.5 0.8 iota_compare_fusion
  241.3 0.7 fusion.21
  242.0 3.6 %compare_select_fusion = f32[512,36]{0,1:T(8,128)S(1)} fusion(bf16[512,4096]{1,0:T(8,128)(2,1)} %all-gather.6.cloned.1.call-done, bf16[4096,36]{0,1:T(8,128)(2,1)S(1)} %copy-done.4), kind=kOutput, calls=%fused_computation.46 | convolution fusion | flops 151105536 | bytes 4562944 | tf_op jit(solution)/shard_map/dot_general | solution.py:44
  245.8 5.9 %convolution_convert_fusion = bf16[512,512]{0,1:T(8,128)(2,1)S(1)} fusion(bf16[512,4096]{1,0:T(8,128)(2,1)} %all-gather.6.cloned.1.call-done, bf16[4096,512]{1,0:T(8,128)(2,1)} %param.11), kind=kOutput, calls=%fused_computation.20 | convolution fusion | flops 2147745792 | bytes 8912896 | tf_op jit(solution)/shard_map/dot_general | solution.py:44
  251.6 2.6 bitcast_multiply_fusion.1
  254.2 1.9 copy-done.1
  256.2 0.7 fusion.4
  256.9 20.4 %fusion = f32[6,4,128,128]{3,0,2,1:T(8,128)S(1)} fusion(f32[64,4,128,128]{3,2,1,0:T(8,128)} %bitcast.101, f32[64,4]{0,1:T(4,128)S(1)} %select_exponential_fusion, s32[64]{0:T(128)S(1)} %fusion.45, pred[64]{0:T(512)(128)(4,1)S(1)} %iota_compare_fusion.2), kind=kOutput, calls=%fused_computation.2 | convolution fusion | flops 306184960 | bytes 18351424 | tf_op jit(solution)/shard_map/nb,nh,nhde->bhde/dot_general | solution.py:101
  277.3 1.0 fusion.23
  278.3 1.2 fusion.2
  279.5 1.0 copy-done.2
  280.5 0.9 multiply_reduce_fusion
  281.4 1.3 copy-done.3
  282.7 4.4 %bitcast_convert_fusion = bf16[512,4096]{1,0:T(8,128)(2,1)} fusion(bf16[4,128,4096]{2,1,0:T(8,128)(2,1)S(1)} %bitcast.102, f32[4,512,128]{1,2,0:T(8,128)S(1)} %get-tuple-element.48, f32[4,512]{1,0:T(4,128)S(1)} %add_rsqrt_fusion), kind=kOutput, calls=%fused_computation.3 | convolution fusion | flops 2150105088 | bytes 9445376 | tf_op jit(solution)/shard_map/htd,hde->te/dot_general | solution.py:119
  287.1 47.8 %reduce-scatter.2.cloned.1.call-done = bf16[512,1024]{1,0:T(8,128)(2,1)} async-done(((bf16[512,4096]{1,0:T(8,128)(2,1)}), bf16[512,1024]{1,0:T(8,128)(2,1)}) %reduce-scatter.2.cloned.1.call-update) | async-done | bytes 1048592 | tf_op jit(solution)/shard_map/reduce_scatter | solution.py:125
  (43 shorter events, 2.4 us)
Async XLA Ops:
  6.5 57.3 %copy-start = (bf16[4096,128]{1,0:T(8,128)(2,1)S(1)}, bf16[4096,128]{1,0:T(8,128)(2,1)}, u32[]{:S(2)}) copy-start(bf16[4096,128]{1,0:T(8,128)(2,1)} %param.12) | copy-start | bytes 3145732
  6.5 57.3 %all-gather.6.cloned.1.call-start = ((), (), s32[]{:S(2)}) async-start(), calls=%async_computation.1 | async-start | bytes 5242880 | tf_op jit(solution)/shard_map/all_gather | solution.py:42
  7.3 249.6 %all-gather.8.cloned.1.call-start = ((), (), s32[]{:S(2)}) async-start(), calls=%async_computation.3 | async-start | bytes 17039360 | tf_op jit(solution)/shard_map/all_gather | solution.py:92
  67.3 5.3 %copy-start.6 = (u32[256]{0:T(256)S(1)}, u32[256]{0:T(256)}, u32[]{:S(2)}) copy-start(u32[256]{0:T(256)} %constant.67) | copy-start | bytes 3076
  67.4 174.6 %copy-start.4 = (bf16[4096,36]{0,1:T(8,128)(2,1)S(1)}, bf16[4096,36]{0,1:T(8,128)(2,1)}, u32[]{:S(2)}) copy-start(bf16[4096,36]{0,1:T(8,128)(2,1)} %param.14) | copy-start | bytes 884740
  72.5 262.3 %reduce-scatter.2.cloned.1.call-start = ((), (), s32[]{:S(2)}) async-start(), calls=%async_computation.2 | async-start | bytes 5242880 | tf_op jit(solution)/shard_map/reduce_scatter | solution.py:125
  245.7 5.9 %copy-start.5 = (pred[512,512]{0,1:T(8,128)(4,1)S(1)}, pred[512,512]{0,1:T(8,128)(4,1)}, u32[]{:S(2)}) copy-start(pred[512,512]{0,1:T(8,128)(4,1)} %iota_compare_fusion) | copy-start | bytes 786436
  254.2 1.9 copy-start.1
  278.3 2.2 copy-start.2
  280.5 2.2 copy-start.3
Sparse Core Ops, SparseCore 0:
  9.2 54.6 all-gather.5
  72.7 100.9 all-gather.7
  287.2 47.6 reduce-scatter.1
where the time goes:
time: 342 us; the launch traced here: 341 us
  blocking collectives  166 us (49%)
  waiting for transfers between devices  102 us (30%)
  matrix products  49.1 us (14%)
  between operations  14 us (4%)
  local copies, waits for them, and re-layouts  6.27 us (2%)
    unnamed x1, blocking collectives  124 us
    all_gather x1, waiting for transfers between devices, body(): piece = lax.all_gather(tokens, 'tp', axis=1, tiled=True)  53.9 us
    reduce_scatter x1, waiting for transfers between devices, body(): lax.psum_scatter(partial_out.astype(jnp.bfloat16), 'tp', scatter_dimensio...  47.8 us
    all_gather x1, blocking collectives, prefix(): gathered = lax.all_gather(part, axis)  41.7 us
    dot_general x1, matrix products, body(): jnp.einsum('nb,nh,nhde->bhde', onehot, fading, states, precision=HIGHEST)  20.4 us
    dot_general x4, matrix products, body(): jnp.dot(piece, matrix, preferred_element_type=jnp.float32)  16.7 us
  transfers between devices with their start and end apart: 3, of which 2 were waited for; matrix products, arithmetic and copies ran while one was open for 5% of the time, Pallas kernels for 0%

commit v1 on v0

--- a/solution.py
+++ b/solution.py
@@ -5,6 +5,30 @@
 
 BLOCK = 128
 HIGHEST = lax.Precision.HIGHEST
+
+
+def _keep_up_desk(slab_in, where_dim):
+    slab_in = jnp.moveaxis(slab_in, 0, where_dim)
+    local_now = slab_in.shape
+    m_next = slab_in.reshape(
+        *local_now[:where_dim],
+        local_now[where_dim] * local_now[where_dim + 1],
+        *local_now[where_dim + 2 :]
+    )
+    return m_next
+
+
+def carry_the_object(incoming_x, link_axis):
+    opened, tile_out = (lax.axis_size(link_axis), lax.axis_index(link_axis))
+    high, f_next = (incoming_x[None], 1)
+    while f_next < opened:
+        lower = lax.ppermute(high, link_axis, [(w, w ^ f_next) for w in range(opened)])
+        parts_out = tile_out & f_next == 0
+        high = jnp.concatenate(
+            [jnp.where(parts_out, high, lower), jnp.where(parts_out, lower, high)]
+        )
+        f_next *= 2
+    return high
 
 
 def prefix(part, axis, combine, identity):
@@ -39,7 +63,7 @@
     kv_local = w_key.shape[1] // head_size
     group_size = heads_local // kv_local
     matrices = (w_query, w_key, w_value, w_level)
-    piece = lax.all_gather(tokens, "tp", axis=1, tiled=True)
+    piece = _keep_up_desk(carry_the_object(tokens, "tp"), 1)
     sums = tuple(
         (jnp.dot(piece, matrix, preferred_element_type=jnp.float32) for matrix in matrices)
     )

time: 342 us -> 364 us (1.064)
  waiting for transfers between devices: 102 us -> 113 us
  starting transfers between devices: 0.08 us -> 6.37 us
  matrix products: 49.1 us -> 43.9 us
  other arithmetic: 3.27 us -> 8.29 us
  blocking collectives: 166 us -> 170 us
    ppermute x0 -> x2, waiting for transfers between devices: none -> 64.2 us  [carry_the_object(): lax.ppermute(high, link_axis, [(w, w ^ f_next) for w in range(opened)])]
    all_gather x1 -> x0, waiting for transfers between devices: 53.9 us -> none  [body(): piece = lax.all_gather(tokens, 'tp', axis=1, tiled=True)]
    ppermute x0 -> x2, starting transfers between devices: none -> 6.33 us  [carry_the_object(): lax.ppermute(high, link_axis, [(w, w ^ f_next) for w in range(opened)])]
    dot_general x4, matrix products: 16.7 us -> 11.5 us  [body(): jnp.dot(piece, matrix, preferred_element_type=jnp.float32)]
    select_n x0 -> x2, other arithmetic: none -> 3.81 us  [carry_the_object(): jnp.where(parts_out, high, lower)]
  transfers between devices with their start and end apart: 3 -> 4, of which waited for: 2 -> 3; matrix products, arithmetic and copies ran while one was open for 5% -> 4% of each run, Pallas kernels for 0% -> 0%
where the time goes in v1:
time: 364 us
  blocking collectives  170 us (47%)
  waiting for transfers between devices  113 us (31%)
  matrix products  43.9 us (12%)
  between operations  14.3 us (4%)
  other arithmetic  8.29 us (2%)
  local copies, waits for them, and re-layouts  7.91 us (2%)
  starting transfers between devices  6.37 us (2%)
    unnamed x1, blocking collectives  125 us
    ppermute x2, waiting for transfers between devices, carry_the_object(): lax.ppermute(high, link_axis, [(w, w ^ f_next) for w in range(opened)])  64.2 us
    reduce_scatter x1, waiting for transfers between devices, body(): lax.psum_scatter(partial_out.astype(jnp.bfloat16), 'tp', scatter_dimensio...  48.9 us
    all_gather x1, blocking collectives, prefix(): gathered = lax.all_gather(part, axis)  44.9 us
    dot_general x1, matrix products, body(): jnp.einsum('nb,nh,nhde->bhde', onehot, fading, states, precision=HIGHEST)  20.5 us
    dot_general x4, matrix products, body(): jnp.dot(piece, matrix, preferred_element_type=jnp.float32)  11.5 us
  transfers between devices with their start and end apart: 4, of which 3 were waited for; matrix products, arithmetic and copies ran while one was open for 4% of the time, Pallas kernels for 0%

profile of v1, /device:TPU:1, one launch (start us, length us, event | category | flops | bytes accessed | tf_op | source)
XLA Modules:
  0.0 363.6 jit_solution(5326039434960570081)
XLA Ops:
  6.5 1.6 copy.65
  8.1 2.2 collective-permute-start
  10.4 21.6 %collective-permute-done = bf16[1,512,1024]{1,2,0:T(8,128)(2,1)} collective-permute-done((bf16[1,512,1024]{1,2,0:T(8,128)(2,1)S(1)}, bf16[1,512,1024]{1,2,0:T(8,128)(2,1)}, u32[]{:S(2)}, u32[]{:S(2)}) %collective-permute-start) | collective-permute-done | bytes 1048608 | tf_op jit(solution)/shard_map/ppermute | solution.py:25
  32.0 1.7 broadcast_select_fusion.3
  33.7 1.5 pad_maximum_fusion.1
  35.2 4.1 %collective-permute-start.1 = (bf16[2,512,1024]{1,2,0:T(8,128)(2,1)}, bf16[2,512,1024]{1,2,0:T(8,128)(2,1)}, u32[]{:S(2)}, u32[]{:S(2)}) collective-permute-start(bf16[2,512,1024]{1,2,0:T(8,128)(2,1)} %pad_maximum_fusion.1), channel_id=1, source_target_pairs={{0,2},{1,3},{2,0},{3,1},{4,6},{5,7},{6,4},{7,5},{8,10},{9,11},{10,... | collective-permute-start | bytes 6291464 | tf_op jit(solution)/shard_map/ppermute | solution.py:25
  39.3 1.2 reduce-window.6
  41.2 42.6 %collective-permute-done.1 = bf16[2,512,1024]{1,2,0:T(8,128)(2,1)} collective-permute-done((bf16[2,512,1024]{1,2,0:T(8,128)(2,1)}, bf16[2,512,1024]{1,2,0:T(8,128)(2,1)}, u32[]{:S(2)}, u32[]{:S(2)}) %collective-permute-start.1) | collective-permute-done | bytes 2097184 | tf_op jit(solution)/shard_map/ppermute | solution.py:25
  83.8 2.1 broadcast_select_fusion.1
  86.4 1.3 fusion.14
  88.4 1.3 convolution_convert_fusion.2
  92.4 44.9 %all-gather.2 = f32[64,1,4]{2,1,0:T(1,128)S(1)} all-gather(f32[1,1,4]{2,1,0:T(1,128)S(1)} %bitcast.120), channel_id=1, replica_groups=mesh['seq'=64,'tp'=4] {'seq'}, dimensions={0}, use_global_device_ids=true | all-gather | bytes 1040 | tf_op jit(solution)/shard_map/all_gather | solution.py:36
  137.5 124.7 %all-reduce = f32[256]{0:T(256)S(1)} all-reduce(f32[256]{0:T(256)S(1)} %add_dynamic-update-slice_fusion), channel_id=2, replica_groups=mesh['seq'=64,'tp'=4] {'seq'}, use_global_device_ids=true, to_apply=%add | all-reduce | flops 256 | bytes 2048
  263.3 3.0 compare_select_fusion
  266.4 5.8 %convolution_convert_fusion = bf16[512,512]{0,1:T(8,128)(2,1)S(1)} fusion(bf16[512,4096]{0,1:T(8,128)(2,1)} %bitcast.111, bf16[4096,512]{1,0:T(8,128)(2,1)} %param.11), kind=kOutput, calls=%fused_computation.24 | convolution fusion | flops 2147745792 | bytes 8912896 | tf_op jit(solution)/shard_map/dot_general | solution.py:68
  272.3 2.6 bitcast_multiply_fusion.1
  274.9 1.9 copy-done.3
  277.6 20.5 %fusion = f32[6,4,128,128]{3,0,2,1:T(8,128)S(1)} fusion(f32[64,4,128,128]{3,2,1,0:T(8,128)} %bitcast.107, f32[64,4]{0,1:T(4,128)S(1)} %select_exponential_fusion, s32[64]{0:T(128)S(1)} %fusion.45, pred[64]{0:T(512)(128)(4,1)S(1)} %iota_compare_fusion.2), kind=kOutput, calls=%fused_computation.2 | convolution fusion | flops 306184960 | bytes 18351424 | tf_op jit(solution)/shard_map/nb,nh,nhde->bhde/dot_general | solution.py:125
  298.1 1.0 fusion.23
  299.1 1.1 fusion.2
  300.2 1.1 copy-done.4
  302.2 1.3 copy-done.6
  303.5 4.3 %bitcast_convert_fusion = bf16[512,4096]{1,0:T(8,128)(2,1)} fusion(bf16[4,128,4096]{2,1,0:T(8,128)(2,1)S(1)} %bitcast.113, f32[4,512,128]{1,2,0:T(8,128)S(1)} %get-tuple-element.52, f32[4,512]{1,0:T(4,128)S(1)} %add_rsqrt_fusion), kind=kOutput, calls=%fused_computation.3 | convolution fusion | flops 2150105088 | bytes 9445376 | tf_op jit(solution)/shard_map/htd,hde->te/dot_general | solution.py:143
  307.9 48.9 %reduce-scatter.2.cloned.1.call-done = bf16[512,1024]{1,0:T(8,128)(2,1)} async-done(((bf16[512,4096]{1,0:T(8,128)(2,1)}), bf16[512,1024]{1,0:T(8,128)(2,1)}) %reduce-scatter.2.cloned.1.call-update) | async-done | bytes 1048592 | tf_op jit(solution)/shard_map/reduce_scatter | solution.py:149
  (57 shorter events, 6.8 us)
Async XLA Ops:
  6.5 79.8 %copy-start = (bf16[4096,128]{1,0:T(8,128)(2,1)S(1)}, bf16[4096,128]{1,0:T(8,128)(2,1)}, u32[]{:S(2)}) copy-start(bf16[4096,128]{1,0:T(8,128)(2,1)} %param.13) | copy-start | bytes 3145732
  6.5 271.1 %all-gather.5.cloned.1.call-start = ((), (), s32[]{:S(2)}) async-start(), calls=%async_computation.2 | async-start | bytes 17039360 | tf_op jit(solution)/shard_map/all_gather | solution.py:116
  8.1 2.2 copy-start.5
  8.1 23.8 %collective-permute-start = (bf16[1,512,1024]{1,2,0:T(8,128)(2,1)S(1)}, bf16[1,512,1024]{1,2,0:T(8,128)(2,1)}, u32[]{:S(2)}, u32[]{:S(2)}) collective-permute-start(bf16[1,512,1024]{1,2,0:T(8,128)(2,1)S(1)} %bitcast.112), channel_id=1, source_target_pairs={{0,1},{1,0},{2,3},{3,2},{4,5},{5,4},{6,7},{7,6},{8,9},{9,8},{10,11... | collective-permute-start | bytes 3145736 | tf_op jit(solution)/shard_map/ppermute | solution.py:25
  10.4 28.9 %copy-start.8 = (f32[512,4]{0,1:T(4,128)S(1)}, f32[512,4]{0,1:T(4,128)}, u32[]{:S(2)}) copy-start(f32[512,4]{0,1:T(4,128)} %param.10) | copy-start | bytes 24580
  35.2 48.7 %collective-permute-start.1 = (bf16[2,512,1024]{1,2,0:T(8,128)(2,1)}, bf16[2,512,1024]{1,2,0:T(8,128)(2,1)}, u32[]{:S(2)}, u32[]{:S(2)}) collective-permute-start(bf16[2,512,1024]{1,2,0:T(8,128)(2,1)} %pad_maximum_fusion.1), channel_id=1, source_target_pairs={{0,2},{1,3},{2,0},{3,1},{4,6},{5,7},{6,4},{7,5},{8,10},{9,11},{10,... | collective-permute-start | bytes 6291464 | tf_op jit(solution)/shard_map/ppermute | solution.py:25
  86.3 1.9 copy-start.2
  86.4 2.0 copy-start.9
  88.4 2.8 copy-start.10
  88.4 174.9 %copy-start.7 = (bf16[4096,36]{0,1:T(8,128)(2,1)S(1)}, bf16[4096,36]{0,1:T(8,128)(2,1)}, u32[]{:S(2)}) copy-start(bf16[4096,36]{0,1:T(8,128)(2,1)} %param.14) | copy-start | bytes 884740
  91.1 265.6 %reduce-scatter.2.cloned.1.call-start = ((), (), s32[]{:S(2)}) async-start(), calls=%async_computation.1 | async-start | bytes 5242880 | tf_op jit(solution)/shard_map/reduce_scatter | solution.py:149
  274.9 1.9 copy-start.3
  299.1 2.2 copy-start.4
  301.3 2.2 copy-start.6
  303.5 53.2 %copy-start.1 = (bf16[4096,128]{1,0:T(8,128)(2,1)S(1)}, bf16[4096,128]{1,0:T(8,128)(2,1)}, u32[]{:S(2)}) copy-start(bf16[4096,128]{1,0:T(8,128)(2,1)} %param.13) | copy-start | bytes 3145732
Sparse Core Ops, SparseCore 0:
  91.3 105.4 all-gather.4
  308.0 48.6 reduce-scatter.1
